TPU v7x, 256 devices: a whole 4x4x8 slice. The times are simulated.
256 devices in a mesh: cache: 32 (over x, y, core), mp: 8 (over z).
Axes of the slice: x: 4, y: 4, z: 8, core: 2. Of those that a mesh axis runs over, the one named last changes fastest.
Arguments:
- cand_rows: bfloat16 [32768, 1024], P('cache', 'mp'), may hold values from -6 to 6
- w_in: bfloat16 [1024, 8, 256], P(None, 'mp'), may hold values from -0.1875 to 0.1875
- w_out: bfloat16 [8, 128, 1024], P('mp'), may hold values from -0.25 to 0.25
- kv_pool: bfloat16 [2, 4096, 128, 1024], P(None, 'cache', None, 'mp'), may hold values from -6 to 6
- send_list: int32 [32, 128], P('cache'), may hold values from 0 to 127, each once within a row
- block_live: int32 [32, 128], P('cache'), may hold values from 0 to 1, as said below
- cand_count: int32 [32], P('cache'), may hold values from 128 to 1024, as said below
Outputs:
- ranked: bfloat16 [32768, 1024], P('cache', 'mp')
Inputs may be any that keep to these rules, and one draw needn't show every extreme that they name: `block_live`: among the 4 slots that one owner keeps for one ranker at most 2 are live; some ranker has exactly 2 live slots from every owner. `cand_count`: some ranker has exactly 1024 live rows. `send_list`: each row is a permutation of the owner's 128 pool blocks.
All inputs are finite; a program needn't handle non-finite values.
Results may differ from a plain program's by a relative error of at most 0.015.
Values may be sent and summed in bfloat16 or wider, within the bound.
No kernel may reach another device: no remote copies, remote signals or barrier semaphores. Data moves between devices by JAX's collectives and lax.ppermute only.
A program may use at most 128 MiB of HBM per device.

v0:
```python
import math

import jax
import jax.numpy as jnp
from jax import lax
from jax.sharding import PartitionSpec as P


def per_device(cand_rows, w_in, w_out, kv_pool, send_list, block_live, cand_count):
    tok_rows = cand_rows.shape[0]
    heads_here = w_in.shape[1]
    head_size = w_in.shape[2] // 2
    block_len = kv_pool.shape[2]
    width = kv_pool.shape[3]
    rankers = lax.axis_size("cache")
    w_flat = w_in.reshape(w_in.shape[0], -1)
    proj = jnp.dot(
        lax.all_gather(cand_rows, "mp", axis=1, tiled=True),
        w_flat,
        preferred_element_type=jnp.float32,
    )
    proj = proj.reshape(tok_rows, heads_here, 2 * head_size)
    gate = jax.nn.silu(proj[..., :head_size])
    query = jax.nn.silu(proj[..., head_size:]).astype(jnp.bfloat16)
    local = send_list.reshape(rankers, -1)
    live = block_live.reshape(rankers, -1)
    outgoing = kv_pool[:, local.reshape(-1)] * live.reshape(-1)[None, :, None, None].astype(
        jnp.bfloat16
    )
    outgoing = outgoing.reshape(2, rankers, local.shape[1], block_len, width)
    arrived = lax.all_to_all(outgoing, "cache", split_axis=1, concat_axis=1, tiled=True)
    history = arrived.reshape(2, -1, heads_here, head_size)
    key_total = history.shape[1]
    step_keys = math.gcd(key_total, 4096)
    scale = head_size ** (-0.5)

    def accumulate(turn, total):
        pair = lax.dynamic_slice_in_dim(history, turn * step_keys, step_keys, 1)
        score = (
            jnp.einsum("thd,khd->thk", query, pair[0], preferred_element_type=jnp.float32) * scale
        )
        weight = jax.nn.silu(score).astype(jnp.bfloat16)
        return total + jnp.einsum(
            "thk,khd->thd", weight, pair[1], preferred_element_type=jnp.float32
        )

    attended = lax.fori_loop(
        0,
        key_total // step_keys,
        accumulate,
        jnp.zeros((tok_rows, heads_here, head_size), jnp.float32),
    )
    center = attended - jnp.mean(attended, axis=-1, keepdims=True)
    variance = jnp.mean(center * center, axis=-1, keepdims=True)
    gated = (center / jnp.sqrt(variance + 1e-05) * gate).astype(jnp.bfloat16)
    partial_term = jnp.dot(
        gated.reshape(tok_rows, -1),
        w_out.reshape(-1, w_out.shape[2]),
        preferred_element_type=jnp.float32,
    )
    summed = lax.psum_scatter(
        partial_term.astype(jnp.bfloat16), "mp", scatter_dimension=1, tiled=True
    ).astype(jnp.float32)
    keep = (jnp.arange(tok_rows, dtype=jnp.int32) < cand_count[0])[:, None]
    return jnp.where(keep, cand_rows.astype(jnp.float32) + summed, jnp.float32(0.0)).astype(
        jnp.bfloat16
    )


def solution(mesh):
    return jax.shard_map(
        per_device,
        mesh=mesh,
        in_specs=(
            P("cache", "mp"),
            P(None, "mp", None),
            P("mp", None, None),
            P(None, "cache", None, "mp"),
            P("cache", None),
            P("cache", None),
            P("cache"),
        ),
        out_specs=P("cache", "mp"),
        check_vma=False,
    )
```

profile of v0, /device:TPU:104, one launch (start us, length us, event | category | flops | bytes accessed | tf_op | source)
XLA Modules:
  0.0 276.4 jit_solution(10782728872227148917)
XLA Ops:
  6.5 0.0 copy-start
  6.5 0.7 fusion.23
  7.3 10.0 %gather_fusion = bf16[128,2,128,128]{3,2,1,0:T(8,128)(2,1)} fusion(bf16[2,128,128,128]{3,2,1,0:T(8,128)(2,1)} %param.12, s32[1024]{0:T(1024)S(1)} %pad_clamp_fusion), kind=kCustom, calls=%fused_computation | custom fusion | bytes 16777728 | tf_op jit(solution)/shard_map/gather | solution.py:27
  17.2 0.0 copy-start.4
  17.2 10.4 %copy.21 = bf16[2,128,128,128]{3,2,1,0:T(8,128)(2,1)} copy(bf16[2,128,128,128]{3,2,0,1:T(8,128)(2,1)} %bitcast.84) | data formatting | bytes 16777216 | tf_op jit(solution)/shard_map/gather | solution.py:27
  27.6 0.0 copy-done.4
  27.6 0.1 convert_element_type.38
  27.7 7.6 %broadcast_multiply_fusion = bf16[2,32,4,128,128]{4,3,2,1,0:T(8,128)(2,1)} fusion(bf16[2,32,4,128,128]{4,3,2,1,0:T(8,128)(2,1)} %bitcast.85, bf16[32,4]{1,0:T(8,128)(2,1)S(1)} %convert_element_type.38), kind=kLoop, calls=%fused_computation.17 | loop fusion | flops 4194304 | bytes 16777472 | tf_op jit(solution)/shard_map/mul | solution.py:27
  35.3 10.3 %copy.22 = bf16[2,32,4,128,128]{4,3,2,0,1:T(8,128)(2,1)} copy(bf16[2,32,4,128,128]{4,3,2,1,0:T(8,128)(2,1)} %broadcast_multiply_fusion) | data formatting | bytes 16777216 | tf_op jit(solution)/shard_map/mul | solution.py:27
  45.6 7.6 %all-to-all-start = ((bf16[2,32,4,128,128]{4,3,2,0,1:T(8,128)(2,1)}), bf16[2,32,4,128,128]{4,3,2,0,1:T(8,128)(2,1)}, u32[]{:S(2)}, u32[]{:S(2)}) async-start(bf16[2,32,4,128,128]{4,3,2,0,1:T(8,128)(2,1)} %copy.22), calls=%async_computation | async-start | bytes 16777216 | tf_op jit(solution)/shard_map/all_to_all | solution.py:31
  53.2 0.0 all-gather.2.cloned.1.call-start
  53.3 0.7 all-gather.2.cloned.1.call-update
  54.0 0.2 reduce-scatter.4.cloned.1.call-start
  54.2 48.8 %all-gather.2.cloned.1.call-done = bf16[1024,1024]{1,0:T(8,128)(2,1)} async-done(((bf16[1024,128]{1,0:T(8,128)(2,1)}), bf16[1024,1024]{1,0:T(8,128)(2,1)}) %all-gather.2.cloned.1.call-update) | async-done | bytes 2097168 | tf_op jit(solution)/shard_map/all_gather | solution.py:18
  103.0 0.0 copy-done
  103.0 2.3 convolution_bitcast_fusion
  105.3 0.0 copy-start.3
  105.3 1.0 copy-done.3
  106.3 0.1 multiply_convert_fusion.1
  106.5 71.0 %all-to-all-done = bf16[2,32,4,128,128]{4,3,2,0,1:T(8,128)(2,1)} async-done(((bf16[2,32,4,128,128]{4,3,2,0,1:T(8,128)(2,1)}), bf16[2,32,4,128,128]{4,3,2,0,1:T(8,128)(2,1)}, u32[]{:S(2)}, u32[]{:S(2)}) %all-to-all-start) | async-done | bytes 8388640 | tf_op jit(solution)/shard_map/all_to_all | solution.py:31
  177.5 10.3 %copy.23 = bf16[2,32,4,128,128]{4,3,2,1,0:T(8,128)(2,1)} copy(bf16[2,32,4,128,128]{4,3,2,0,1:T(8,128)(2,1)} %all-to-all-done) | data formatting | bytes 16777216 | tf_op jit(solution)/shard_map/all_to_all | solution.py:31
  187.8 32.8 %while.14 = (s32[]{:T(128)}, f32[1024,1,128]{0,2,1:T(8,128)S(1)}, bf16[2,16384,1,128]{3,1,2,0:T(8,128)(2,1)}, bf16[1024,1,128]{2,0,1:T(8,128)(2,1)S(1)}, s32[]{:...) while((s32[]{:T(128)}, f32[1024,1,128]{0,2,1:T(8,128)S(1)}, ...), condition=%wide.region_1.2_spmd.clone, body=%wide.region_0.1_spmd.clone.sunk | while | flops 2172911616 | bytes 3410080 | solution.py:47
  187.8 8.2 %fusion.31 = f32[1024,1,128]{0,2,1:T(8,128)S(1)} fusion(bf16[2,16384,1,128]{3,1,2,0:T(8,128)(2,1)} %get-tuple-element.173, s32[]{:T(128)S(6)} %select_n.29, s32[]{:T(128)S(6)} %add.126, f32[1024,1,128]{0,2,1:T(8,128)S(1)} %get-tuple-element.163, bf16[1024,1,128]{2,0,1:T(8,128)(2,1)S(1)} %get-tuple-element.174, pred[]{:T(512)S(6)} %compare.3), kind=kOutput, calls=%fused_computation.10.clone.1 | convolution fusion | flops 2172911616 | bytes 3409920 | tf_op jit(solution)/shard_map/while/body/eval_jaxpr/thk,khd->thd/dot_general | solution.py:43
  196.0 8.2 %fusion.31 = f32[1024,1,128]{0,2,1:T(8,128)S(1)} fusion(bf16[2,16384,1,128]{3,1,2,0:T(8,128)(2,1)} %get-tuple-element.173, s32[]{:T(128)S(6)} %select_n.29, s32[]{:T(128)S(6)} %add.126, f32[1024,1,128]{0,2,1:T(8,128)S(1)} %get-tuple-element.163, bf16[1024,1,128]{2,0,1:T(8,128)(2,1)S(1)} %get-tuple-element.174, pred[]{:T(512)S(6)} %compare.3), kind=kOutput, calls=%fused_computation.10.clone.1 | convolution fusion | flops 2172911616 | bytes 3409920 | tf_op jit(solution)/shard_map/while/body/eval_jaxpr/thk,khd->thd/dot_general | solution.py:43
  204.2 8.2 %fusion.31 = f32[1024,1,128]{0,2,1:T(8,128)S(1)} fusion(bf16[2,16384,1,128]{3,1,2,0:T(8,128)(2,1)} %get-tuple-element.173, s32[]{:T(128)S(6)} %select_n.29, s32[]{:T(128)S(6)} %add.126, f32[1024,1,128]{0,2,1:T(8,128)S(1)} %get-tuple-element.163, bf16[1024,1,128]{2,0,1:T(8,128)(2,1)S(1)} %get-tuple-element.174, pred[]{:T(512)S(6)} %compare.3), kind=kOutput, calls=%fused_computation.10.clone.1 | convolution fusion | flops 2172911616 | bytes 3409920 | tf_op jit(solution)/shard_map/while/body/eval_jaxpr/thk,khd->thd/dot_general | solution.py:43
  212.4 8.2 %fusion.31 = f32[1024,1,128]{0,2,1:T(8,128)S(1)} fusion(bf16[2,16384,1,128]{3,1,2,0:T(8,128)(2,1)} %get-tuple-element.173, s32[]{:T(128)S(6)} %select_n.29, s32[]{:T(128)S(6)} %add.126, f32[1024,1,128]{0,2,1:T(8,128)S(1)} %get-tuple-element.163, bf16[1024,1,128]{2,0,1:T(8,128)(2,1)S(1)} %get-tuple-element.174, pred[]{:T(512)S(6)} %compare.3), kind=kOutput, calls=%fused_computation.10.clone.1 | convolution fusion | flops 2172911616 | bytes 3409920 | tf_op jit(solution)/shard_map/while/body/eval_jaxpr/thk,khd->thd/dot_general | solution.py:43
  220.6 0.0 copy-start.2
  220.6 0.0 copy-start.1
  220.6 0.2 copy.25
  220.9 0.4 multiply_reduce_fusion
  221.3 1.9 convolution_convert_fusion
  223.2 2.6 copy.26
  225.7 0.0 reduce-scatter.4.cloned.1.call-update
  226.4 41.1 %reduce-scatter.4.cloned.1.call-done = bf16[128,1024]{1,0:T(8,128)(2,1)} async-done(((bf16[1024,1024]{1,0:T(8,128)(2,1)}), bf16[128,1024]{1,0:T(8,128)(2,1)}) %reduce-scatter.4.cloned.1.call-update) | async-done | bytes 262160
  267.5 1.1 copy.27
  268.6 0.0 copy-done.2
  268.7 0.9 select_convert_fusion
  269.6 0.0 copy-done.1
  (7 shorter events, 0.1 us)
Async XLA Ops:
  6.5 96.5 %copy-start = (bf16[1024,1,256]{2,0,1:T(8,128)(2,1)S(1)}, bf16[1024,1,256]{2,0,1:T(8,128)(2,1)}, u32[]{:S(2)}) copy-start(bf16[1024,1,256]{2,0,1:T(8,128)(2,1)} %param.10) | copy-start | bytes 1572868
  17.2 10.4 %copy-start.4 = (s32[1,128]{1,0:T(1,128)S(1)}, s32[1,128]{1,0:T(1,128)}, u32[]{:S(2)}) copy-start(s32[1,128]{1,0:T(1,128)} %param.14) | copy-start | bytes 1540
  45.6 131.9 %all-to-all-start = ((bf16[2,32,4,128,128]{4,3,2,0,1:T(8,128)(2,1)}), bf16[2,32,4,128,128]{4,3,2,0,1:T(8,128)(2,1)}, u32[]{:S(2)}, u32[]{:S(2)}) async-start(bf16[2,32,4,128,128]{4,3,2,0,1:T(8,128)(2,1)} %copy.22), calls=%async_computation | async-start | bytes 16777216 | tf_op jit(solution)/shard_map/all_to_all | solution.py:31
  53.2 49.8 %all-gather.2.cloned.1.call-start = ((), (), s32[]{:S(2)}) async-start(), calls=%async_computation.2 | async-start | bytes 2359296 | tf_op jit(solution)/shard_map/all_gather | solution.py:18
  54.0 213.6 %reduce-scatter.4.cloned.1.call-start = ((), (), s32[]{:S(2)}) async-start(), calls=%async_computation.3 | async-start | bytes 2359296
  105.3 1.0 copy-start.3
  220.6 48.0 %copy-start.2 = (bf16[1024,128]{1,0:T(8,128)(2,1)S(1)}, bf16[1024,128]{1,0:T(8,128)(2,1)}, u32[]{:S(2)}) copy-start(bf16[1024,128]{1,0:T(8,128)(2,1)} %param.9) | copy-start | bytes 786436
  220.6 49.0 %copy-start.1 = (bf16[1024,1,256]{2,0,1:T(8,128)(2,1)S(1)}, bf16[1024,1,256]{2,0,1:T(8,128)(2,1)}, u32[]{:S(2)}) copy-start(bf16[1024,1,256]{2,0,1:T(8,128)(2,1)} %param.10) | copy-start | bytes 1572868
Sparse Core Ops, SparseCore 0:
  55.8 47.1 all-gather.1
  225.9 41.5 reduce-scatter.3
where the time goes:
time: 278 us; the launch traced here: 276 us
  waiting for transfers between devices  162 us (58%)
  local copies, waits for them, and re-layouts  46 us (17%)
  matrix products  36.9 us (13%)
  between operations  14.2 us (5%)
  other arithmetic  9.8 us (4%)
  starting transfers between devices  7.85 us (3%)
    all_to_all x1, waiting for transfers between devices, per_device(): lax.all_to_all(outgoing, 'cache', split_axis=1, concat_axis=1, tiled=True)  71 us
    all_gather x1, waiting for transfers between devices, per_device(): lax.all_gather(cand_rows, 'mp', axis=1, tiled=True)  48.8 us
    unnamed x3, waiting for transfers between devices  41.8 us
    dot_general x4, matrix products, accumulate(): jnp.einsum('thk,khd->thd', weight, pair[1], preferred_element_type=jnp.fl...  32.7 us
    gather x2, local copies, waits for them, and re-layouts, per_device(): kv_pool[:, local.reshape(-1)]  20.3 us
    all_to_all x1, local copies, waits for them, and re-layouts, per_device(): lax.all_to_all(outgoing, 'cache', split_axis=1, concat_axis=1, tiled=True)  10.3 us
    mul x1, local copies, waits for them, and re-layouts, per_device(): kv_pool[:, local.reshape(-1)]  10.3 us
    all_to_all x1, starting transfers between devices, per_device(): lax.all_to_all(outgoing, 'cache', split_axis=1, concat_axis=1, tiled=True)  7.59 us
  transfers between devices with their start and end apart: 3, of which 3 were waited for; matrix products, arithmetic and copies ran while one was open for 1% of the time, Pallas kernels for 0%

commit v1 on v0

v1 whole, which is shorter than its diff:
```python
import jax
import jax.numpy as jnp
from jax import lax
from jax.experimental import pallas as pl
from jax.experimental.pallas import tpu as pltpu
from jax.sharding import PartitionSpec as P

BF16 = jnp.bfloat16
F32 = jnp.float32
VMEM = 16 * 1024 * 1024
LIVE = 2
PARTS = 2


def pack_live(send_list, block_live, kv_pool):
    pool = kv_pool.shape[1]
    tile = kv_pool.shape[2:]
    rankers = lax.axis_size("cache")
    slots = pool // rankers

    def body(send_hbm, live_hbm, pool_ref, out_ref, send_ref, live_ref, sem, list_sem):
        lists = [
            pltpu.make_async_copy(send_hbm, send_ref, list_sem.at[0]),
            pltpu.make_async_copy(live_hbm, live_ref, list_sem.at[1]),
        ]
        for copy in lists:
            copy.start()
        for copy in lists:
            copy.wait()

        def one(r, copies):
            seen = jnp.int32(0)
            blocks = [jnp.int32(0)] * LIVE
            for s in range(slots):
                live = live_ref[0, r * slots + s]
                for k in range(LIVE):
                    hit = jnp.logical_and(seen == k, live > 0)
                    blocks[k] = jnp.where(hit, send_ref[0, r * slots + s], blocks[k])
                seen = seen + live
            for k in range(LIVE):

                @pl.when(seen > k)
                def _():
                    pltpu.make_async_copy(
                        pool_ref.at[:, blocks[k]], out_ref.at[r, pl.ds(2 * k, 2)], sem
                    ).start()

                @pl.when(seen <= k)
                def _():
                    out_ref[r, pl.ds(2 * k, 2)] = jnp.zeros((2,) + tile, BF16)

            return copies + jnp.minimum(seen, LIVE)

        def done(_, carry):
            half = out_ref.at[0, pl.ds(0, 2)]
            pltpu.make_async_copy(half, half, sem).wait()
            return carry

        copies = lax.fori_loop(0, rankers, one, jnp.int32(0), unroll=4)
        lax.fori_loop(0, copies, done, 0)

    hbm = pl.BlockSpec(memory_space=pltpu.HBM)
    return pl.pallas_call(
        body,
        out_shape=jax.ShapeDtypeStruct((rankers, 2 * LIVE) + tile, BF16),
        in_specs=[hbm, hbm, hbm],
        out_specs=pl.BlockSpec(memory_space=pltpu.VMEM),
        scratch_shapes=[
            pltpu.SMEM(send_list.shape, jnp.int32),
            pltpu.SMEM(block_live.shape, jnp.int32),
            pltpu.SemaphoreType.DMA,
            pltpu.SemaphoreType.DMA((2,)),
        ],
        compiler_params=pltpu.CompilerParams(vmem_limit_bytes=VMEM),
        name="pack_live",
    )(send_list, block_live, kv_pool)


def stage(place, cand_rows, w_out):
    n = lax.axis_size("mp")
    rows, width = cand_rows.shape
    depth = w_out.shape[0]
    half = depth // 2
    total = rows + half + (n // 2 - 1) * depth

    def body(place_ref, rows_ref, w_ref, up_ref, down_ref, sem):
        def weights(k):
            start = pl.multiple_of(lax.rem(place_ref[0] + (k + n), n) * width, width)
            return w_ref.at[:, pl.ds(start, width)]

        copies = [
            (rows_ref, up_ref.at[pl.ds(half, rows)]),
            (rows_ref, down_ref.at[pl.ds(0, rows)]),
            (weights(n // 2).at[pl.ds(0, half)], up_ref.at[pl.ds(0, half)]),
            (weights(n // 2).at[pl.ds(half, half)], down_ref.at[pl.ds(rows, half)]),
        ]
        for k in range(1, n // 2):
            at = pl.ds(total - k * depth, depth)
            copies += [(weights(k), up_ref.at[at]), (weights(-k), down_ref.at[at])]
        copies = [pltpu.make_async_copy(a, b, sem.at[i]) for i, (a, b) in enumerate(copies)]
        for copy in copies:
            copy.start()
        for copy in copies:
            copy.wait()

    hbm = pl.BlockSpec(memory_space=pltpu.HBM)
    vmem = pl.BlockSpec(memory_space=pltpu.VMEM)
    shape = jax.ShapeDtypeStruct((total, width), BF16)
    return pl.pallas_call(
        body,
        out_shape=(shape, shape),
        in_specs=[pl.BlockSpec(memory_space=pltpu.SMEM), hbm, hbm],
        out_specs=(vmem, vmem),
        scratch_shapes=[pltpu.SemaphoreType.DMA((n + 2,))],
        compiler_params=pltpu.CompilerParams(vmem_limit_bytes=VMEM),
        name="stage",
    )(place, cand_rows, w_out)


def feature_rings(place, cand_rows, w_out):
    n = lax.axis_size("mp")
    rows = cand_rows.shape[0]
    depth = w_out.shape[0]
    half = depth // 2
    up = [(i, (i + 1) % n) for i in range(n)]
    down = [(i, (i - 1) % n) for i in range(n)]
    a, b = stage(place, cand_rows, w_out)
    ups, downs = [], []
    for k in range(n // 2 - 1):
        a = lax.ppermute(a, "mp", up)
        b = lax.ppermute(b, "mp", down)
        ups.append(a)
        downs.append(b)
        if k < n // 2 - 2:
            a, b = a[:-depth], b[:-depth]
    a = lax.ppermute(a[: half + rows // 2], "mp", up)
    b = lax.ppermute(b[rows // 2 : rows + half], "mp", down)
    return ups + [a], downs + [b]


def ring_gather(x, axis):
    n = lax.axis_size(axis)
    up = [(i, (i + 1) % n) for i in range(n)]
    down = [(i, (i - 1) % n) for i in range(n)]
    got = [x]
    left = right = x
    for _ in range(n // 2 - 1):
        left = lax.ppermute(left, axis, up)
        right = lax.ppermute(right, axis, down)
        got += [right, left]
    half = x.shape[0] // 2
    top = lax.ppermute(left[:half], axis, up)
    bottom = lax.ppermute(right[half:], axis, down)
    return got, top, bottom


def offsets(n):
    order = [0]
    for s in range(1, n // 2):
        order += [s, -s]
    return order + [n // 2]


def project(place, cand_rows, w_out, ups, downs, w_in, scale):
    n = lax.axis_size("mp")
    rows, width = cand_rows.shape
    depth = w_out.shape[0]
    half = depth // 2
    cols = w_in.shape[1]
    tile = rows // 4
    far = n // 2

    def body(*refs):
        place_ref, rows_ref, w_out_ref, w_in_hbm = refs[:4]
        up_refs, down_refs = refs[4 : 4 + far], refs[4 + far : 4 + 2 * far]
        gate_ref, query_ref, w_mine_ref, x_ref, w_in_ref, sem = refs[4 + 2 * far :]

        def spot(k):
            return lax.rem(place_ref[0] + (k + n), n)

        def columns(k):
            return pl.ds(pl.multiple_of(spot(k) * width, width), width)

        def weight_rows(k, start, size):
            return w_mine_ref.at[pl.ds(pl.multiple_of(spot(k) * depth + start, half), size)]

        copies = [
            (w_in_hbm, w_in_ref),
            (rows_ref, x_ref.at[:, columns(0)]),
            (w_out_ref.at[:, columns(0)], weight_rows(0, 0, depth)),
        ]
        for k in range(1, far):
            last = pl.ds(rows + half + (far - 1 - k) * depth, depth)
            copies += [
                (up_refs[k - 1].at[pl.ds(half, rows)], x_ref.at[:, columns(-k)]),
                (up_refs[k - 1].at[last], weight_rows(-k, 0, depth)),
                (down_refs[k - 1].at[pl.ds(0, rows)], x_ref.at[:, columns(k)]),
                (down_refs[k - 1].at[last], weight_rows(k, 0, depth)),
            ]
        top, bottom = pl.ds(0, rows // 2), pl.ds(rows // 2, rows // 2)
        copies += [
            (up_refs[-1].at[pl.ds(half, rows // 2)], x_ref.at[top, columns(far)]),
            (up_refs[-1].at[pl.ds(0, half)], weight_rows(far, 0, half)),
            (down_refs[-1].at[pl.ds(0, rows // 2)], x_ref.at[bottom, columns(far)]),
            (down_refs[-1].at[pl.ds(rows // 2, half)], weight_rows(far, half, half)),
        ]
        copies = [pltpu.make_async_copy(a, b, sem.at[i]) for i, (a, b) in enumerate(copies)]
        for copy in copies:
            copy.start()
        for copy in copies:
            copy.wait()
        for t in range(rows // tile):
            here = pl.ds(t * tile, tile)
            total = jnp.dot(x_ref[here, :], w_in_ref[...], preferred_element_type=F32)
            gate = total[:, : cols // 2]
            query = total[:, cols // 2 :]
            gate_ref[here, :] = gate / (1.0 + jnp.exp(-gate))
            query_ref[here, :] = (query / (1.0 + jnp.exp(-query)) * scale).astype(BF16)

    vmem = pl.BlockSpec(memory_space=pltpu.VMEM)
    hbm = pl.BlockSpec(memory_space=pltpu.HBM)
    return pl.pallas_call(
        body,
        out_shape=(
            jax.ShapeDtypeStruct((rows, cols // 2), F32),
            jax.ShapeDtypeStruct((rows, cols // 2), BF16),
            jax.ShapeDtypeStruct((n * depth, width), BF16),
        ),
        in_specs=[pl.BlockSpec(memory_space=pltpu.SMEM)] + [hbm] * (3 + 2 * far),
        out_specs=(vmem, vmem, vmem),
        scratch_shapes=[
            pltpu.VMEM((rows, n * width), BF16),
            pltpu.VMEM(w_in.shape, BF16),
            pltpu.SemaphoreType.DMA((3 + 4 * far,)),
        ],
        compiler_params=pltpu.CompilerParams(vmem_limit_bytes=VMEM),
        cost_estimate=pl.CostEstimate(
            flops=2 * rows * n * width * cols, bytes_accessed=4 << 20, transcendentals=rows * cols
        ),
        name="project",
    )(place, cand_rows, w_out, w_in, *ups, *downs)


def attend(part, count, query, gate, history):
    at, rows = part
    head = query.shape[1]
    owners, fields, block_len, _ = history.shape
    group = 4
    tile = 256

    def body(count_ref, query_ref, gate_ref, history_ref, out_ref, total_ref):
        step = pl.program_id(0)
        live = jnp.clip(count_ref[0] - at, 0, rows)
        tiles = lax.div(live + (tile - 1), tile)

        @pl.when(step == 0)
        def _():
            total_ref[...] = jnp.zeros_like(total_ref)

        def one(t, _):
            here = pl.ds(pl.multiple_of(t * tile, tile), tile)
            query = query_ref[pl.ds(pl.multiple_of(at + t * tile, tile), tile), :]
            total = total_ref[here, :]
            for k in range(fields // 2):
                keys = history_ref[:, 2 * k].reshape(group * block_len, head)
                values = history_ref[:, 2 * k + 1].reshape(group * block_len, head)
                half = lax.dot_general(
                    query, keys, (((1,), (1,)), ((), ())), preferred_element_type=F32
                )
                weight = (half * jnp.tanh(half) + half).astype(BF16)
                total += jnp.dot(weight, values, preferred_element_type=F32)
            total_ref[here, :] = total
            return 0

        lax.fori_loop(0, tiles, one, 0)

        @pl.when(step == pl.num_programs(0) - 1)
        def _():
            total = total_ref[...]
            center = total - jnp.mean(total, axis=-1, keepdims=True)
            variance = jnp.mean(center * center, axis=-1, keepdims=True)
            scaled = center * lax.rsqrt(variance + 1e-05)
            out_ref[...] = (scaled * gate_ref[pl.ds(at, rows), :]).astype(BF16)

    vmem = pl.BlockSpec(memory_space=pltpu.VMEM)
    keys_all = owners * block_len * fields // 2
    return pl.pallas_call(
        body,
        grid=(owners // group,),
        out_shape=jax.ShapeDtypeStruct((rows, head), BF16),
        in_specs=[
            pl.BlockSpec(memory_space=pltpu.SMEM),
            vmem,
            vmem,
            pl.BlockSpec((group, fields, block_len, head), lambda i: (i, 0, 0, 0)),
        ],
        out_specs=vmem,
        scratch_shapes=[pltpu.VMEM((rows, head), F32)],
        compiler_params=pltpu.CompilerParams(vmem_limit_bytes=VMEM),
        cost_estimate=pl.CostEstimate(
            flops=4 * rows * keys_all * head,
            bytes_accessed=4 << 20,
            transcendentals=rows * keys_all,
        ),
        name="attend",
    )(count, query, gate, history)


def output(place, count, cand_rows, parts, w_mine):
    n = lax.axis_size("mp")
    rows, width = cand_rows.shape
    size = rows // len(parts)
    tile = min(256, size // 2)
    steps = offsets(n)
    each = n + 1

    def body(*refs):
        place_ref, count_ref, rows_ref, w_ref = refs[:4]
        out_ref = refs[-1]
        weights = []
        for s in steps:
            start = lax.rem(place_ref[0] + (s + n), n) * width
            weights.append(w_ref[pl.ds(pl.multiple_of(start, width), width), :])
        for p in range(len(parts)):
            block_refs = refs[4 + p * each : 4 + (p + 1) * each]
            top_ref, bottom_ref = block_refs[-2:]
            for t in range(size // tile):
                local = pl.ds(t * tile, tile)
                here = pl.ds(p * size + t * tile, tile)
                total = rows_ref[here, :].astype(F32)
                for ref, w in zip(block_refs[:-2], weights):
                    total += jnp.dot(ref[local, :], w, preferred_element_type=F32)
                far = top_ref if t * tile < size // 2 else bottom_ref
                last = far[pl.ds((t * tile) % (size // 2), tile), :]
                total += jnp.dot(last, weights[-1], preferred_element_type=F32)
                index = lax.broadcasted_iota(jnp.int32, (tile, width), 0) + (p * size + t * tile)
                out_ref[here, :] = jnp.where(index < count_ref[0], total, 0.0).astype(BF16)

    vmem = pl.BlockSpec(memory_space=pltpu.VMEM)
    smem = pl.BlockSpec(memory_space=pltpu.SMEM)
    blocks = []
    for got, top, bottom in parts:
        blocks += got + [top, bottom]
    return pl.pallas_call(
        body,
        out_shape=jax.ShapeDtypeStruct((rows, width), BF16),
        in_specs=[smem, smem] + [vmem] * (2 + len(blocks)),
        out_specs=vmem,
        compiler_params=pltpu.CompilerParams(vmem_limit_bytes=VMEM),
        cost_estimate=pl.CostEstimate(
            flops=2 * rows * n * width * width, bytes_accessed=4 << 20, transcendentals=0
        ),
        name="output",
    )(place, count, cand_rows, w_mine, *blocks)


def per_device(cand_rows, w_in, w_out, kv_pool, send_list, block_live, cand_count):
    rows = cand_rows.shape[0]
    head = kv_pool.shape[3]
    w_out = w_out.reshape(-1, w_out.shape[2])
    w_in = w_in.reshape(w_in.shape[0], -1)
    place = lax.axis_index("mp").astype(jnp.int32).reshape(1)
    packed = pack_live(send_list, block_live, kv_pool)
    history = lax.all_to_all(packed, "cache", split_axis=0, concat_axis=0, tiled=True)

    cand_later, _ = lax.optimization_barrier((cand_rows, packed))
    ups, downs = feature_rings(place, cand_later, w_out)
    gate, query, w_mine = project(
        place, cand_rows, w_out, ups, downs, w_in, 0.5 * head ** (-0.5)
    )
    size = rows // PARTS
    parts = []
    for p in range(PARTS):
        gated = attend((p * size, size), cand_count, query, gate, history)
        parts.append(ring_gather(gated, "mp"))
    return output(place, cand_count, cand_rows, parts, w_mine)


def solution(mesh):
    return jax.shard_map(
        per_device,
        mesh=mesh,
        in_specs=(
            P("cache", "mp"),
            P(None, "mp", None),
            P("mp", None, None),
            P(None, "cache", None, "mp"),
            P("cache", None),
            P("cache", None),
            P("cache"),
        ),
        out_specs=P("cache", "mp"),
        check_vma=False,
    )
```

time: 278 us -> 123 us (0.44)
  waiting for transfers between devices: 162 us -> 42.8 us
  starting transfers between devices: 7.85 us -> 49.1 us
  local copies, waits for them, and re-layouts: 46 us -> 6.85 us
  matrix products: 36.9 us -> 0 us
  Pallas kernels: 0 us -> 23.3 us
  between operations: 14.2 us -> 0.85 us
  other arithmetic: 9.8 us -> 0 us
    all_to_all x1, waiting for transfers between devices: 71 us -> 10.7 us  [per_device(): lax.all_to_all(packed, 'cache', split_axis=0, concat_axis=0, tiled=True)]
    all_gather x1 -> x0, waiting for transfers between devices: 48.8 us -> none  [per_device(): lax.all_gather(cand_rows, 'mp', axis=1, tiled=True)]
    unnamed x3 -> x0, waiting for transfers between devices: 41.8 us -> none
    ppermute x0 -> x24, starting transfers between devices: none -> 41.5 us  [the longest x6 20 us: ring_gather(): left = lax.ppermute(left, axis, up)]
    dot_general x6 -> x0, matrix products: 36.9 us -> none  [the longest x4 32.7 us: accumulate(): jnp.einsum('thk,khd->thd', weight, pair[1], preferred_element_type=jnp.fl...]
    ppermute x0 -> x24, waiting for transfers between devices: none -> 32.2 us  [the longest x3 20.4 us: feature_rings(): a = lax.ppermute(a, 'mp', up)]
    pallas_call x0 -> x6, Pallas kernels: none -> 23.3 us  [the longest x2 15.8 us: attend(): pl.pallas_call(body, grid=(owners // group,), out_shape=jax.ShapeDtypeStr...]
    gather x2 -> x0, local copies, waits for them, and re-layouts: 20.3 us -> none  [per_device(): kv_pool[:, local.reshape(-1)]]
  transfers between devices with their start and end apart: 3 -> 25, of which waited for: 3 -> 11; matrix products, arithmetic and copies ran while one was open for 1% -> 0% of each run, Pallas kernels for 0% -> 6%
where the time goes in v1:
time: 123 us
  starting transfers between devices  49.1 us (40%)
  waiting for transfers between devices  42.8 us (35%)
  Pallas kernels  23.3 us (19%)
  local copies, waits for them, and re-layouts  6.85 us (6%)
    ppermute x3, waiting for transfers between devices, feature_rings(): a = lax.ppermute(a, 'mp', up)  20.4 us
    ppermute x6, starting transfers between devices, ring_gather(): left = lax.ppermute(left, axis, up)  20 us
    pallas_call x2, Pallas kernels, attend(): pl.pallas_call(body, grid=(owners // group,), out_shape=jax.ShapeDtypeStr...  15.8 us
    ppermute x3, starting transfers between devices, feature_rings(): a = lax.ppermute(a, 'mp', up)  10.7 us
    all_to_all x1, waiting for transfers between devices, per_device(): lax.all_to_all(packed, 'cache', split_axis=0, concat_axis=0, tiled=True)  10.7 us
    all_to_all x1, starting transfers between devices, per_device(): lax.all_to_all(packed, 'cache', split_axis=0, concat_axis=0, tiled=True)  7.68 us
    unnamed x14, local copies, waits for them, and re-layouts  6.71 us
    ppermute x2, starting transfers between devices, ring_gather(): top = lax.ppermute(left[:half], axis, up)  6.6 us
  transfers between devices with their start and end apart: 25, of which 11 were waited for; matrix products, arithmetic and copies ran while one was open for 0% of the time, Pallas kernels for 6%

profile of v1, /device:TPU:104, one launch (start us, length us, event | category | flops | bytes accessed | tf_op | source)
XLA Modules:
  0.0 123.0 jit_solution(15724294884428944829)
XLA Ops:
  0.0 3.4 %copy-done.1 = bf16[2,128,128,128]{3,2,1,0:T(8,128)(2,1)S(1)} copy-done((bf16[2,128,128,128]{3,2,1,0:T(8,128)(2,1)S(1)}, bf16[2,128,128,128]{3,2,1,0:T(8,128)(2,1)}, u32[]{:S(2)}) %copy-start.1) | copy-done | bytes 8388632
  3.4 0.7 copy-done.5
  4.0 0.7 copy-done.6
  4.7 4.0 %pack_live.1 = bf16[32,4,128,128]{3,2,1,0:T(8,128)(2,1)S(1)} custom-call(s32[1,128]{1,0:T(1,128)S(1)} %copy-done.5, s32[1,128]{1,0:T(1,128)S(1)} %copy-done.6, bf16[2,128,128,128]{3,2,1,0:T(8,128)(2,1)S(1)} %copy-done.1), custom_call_target="tpu_custom_call" | custom-call | tf_op jit(solution)/shard_map/pack_live/pallas_call | solution.py:63
  8.7 0.0 copy-start
  8.7 2.0 %copy-done = bf16[32,4,128,128]{3,2,1,0:T(8,128)(2,1)} copy-done((bf16[32,4,128,128]{3,2,1,0:T(8,128)(2,1)}, bf16[32,4,128,128]{3,2,1,0:T(8,128)(2,1)S(1)}, u32[]{:S(2)}) %copy-start) | copy-done | bytes 4194328
  10.7 7.7 %all-to-all-start = ((bf16[32,4,128,128]{3,2,1,0:T(8,128)(2,1)}), bf16[32,4,128,128]{3,2,1,0:T(8,128)(2,1)}, u32[]{:S(2)}, u32[]{:S(2)}) async-start(bf16[32,4,128,128]{3,2,1,0:T(8,128)(2,1)} %copy-done), calls=%async_computation | async-start | bytes 8388608 | tf_op jit(solution)/shard_map/all_to_all | solution.py:364
  18.4 0.0 copy-done.2
  18.4 0.0 copy-done.3
  18.4 0.2 stage.1
  18.7 3.2 %collective-permute-start = (bf16[1472,128]{1,0:T(8,128)(2,1)S(1)}, bf16[1472,128]{1,0:T(8,128)(2,1)S(1)}, u32[]{:S(2)}, u32[]{:S(2)}) collective-permute-start(bf16[1472,128]{1,0:T(8,128)(2,1)S(1)} %get-tuple-element.12), channel_id=1, source_target_pairs={{0,1},{1,2},{2,3},{3,4},{4,5},{5,6},{6,7},{7,0},{8,9},{9,10},{10,1... | collective-permute-start | bytes 1130504 | tf_op jit(solution)/shard_map/ppermute | solution.py:130
  21.9 0.0 collective-permute-start.4
  21.9 8.3 %collective-permute-done.refs_4_ = bf16[1472,128]{1,0:T(8,128)(2,1)S(1)} collective-permute-done((bf16[1472,128]{1,0:T(8,128)(2,1)S(1)}, bf16[1472,128]{1,0:T(8,128)(2,1)S(1)}, u32[]{:S(2)}, u32[]{:S(2)}) %collective-permute-start) | collective-permute-done | bytes 376864 | tf_op jit(solution)/shard_map/ppermute | solution.py:130
  30.2 3.8 %collective-permute-start.1 = (bf16[1344,128]{1,0:T(8,128)(2,1)S(1)}, bf16[1344,128]{1,0:T(8,128)(2,1)S(1)}, u32[]{:S(2)}, u32[]{:S(2)}) collective-permute-start(bf16[1344,128]{1,0:T(8,128)(2,1)S(1)} %slice.40), channel_id=1, source_target_pairs={{0,1},{1,2},{2,3},{3,4},{4,5},{5,6},{6,7},{7,0},{8,9},{9,10},{10,1... | collective-permute-start | bytes 1032200 | tf_op jit(solution)/shard_map/ppermute | solution.py:130
  34.0 0.0 collective-permute-done.4.refs_8_
  34.0 0.1 collective-permute-start.5
  34.1 6.8 %collective-permute-done.1.refs_5_ = bf16[1344,128]{1,0:T(8,128)(2,1)S(1)} collective-permute-done((bf16[1344,128]{1,0:T(8,128)(2,1)S(1)}, bf16[1344,128]{1,0:T(8,128)(2,1)S(1)}, u32[]{:S(2)}, u32[]{:S(2)}) %collective-permute-start.1) | collective-permute-done | bytes 344096 | tf_op jit(solution)/shard_map/ppermute | solution.py:130
  41.0 3.8 %collective-permute-start.2 = (bf16[1216,128]{1,0:T(8,128)(2,1)S(1)}, bf16[1216,128]{1,0:T(8,128)(2,1)S(1)}, u32[]{:S(2)}, u32[]{:S(2)}) collective-permute-start(bf16[1216,128]{1,0:T(8,128)(2,1)S(1)} %slice.41), channel_id=1, source_target_pairs={{0,1},{1,2},{2,3},{3,4},{4,5},{5,6},{6,7},{7,0},{8,9},{9,10},{10,1... | collective-permute-start | bytes 933896 | tf_op jit(solution)/shard_map/ppermute | solution.py:130
  44.7 0.0 collective-permute-done.5.refs_9_
  44.8 0.1 collective-permute-start.6
  44.8 5.3 %collective-permute-done.2.refs_6_ = bf16[1216,128]{1,0:T(8,128)(2,1)S(1)} collective-permute-done((bf16[1216,128]{1,0:T(8,128)(2,1)S(1)}, bf16[1216,128]{1,0:T(8,128)(2,1)S(1)}, u32[]{:S(2)}, u32[]{:S(2)}) %collective-permute-start.2) | collective-permute-done | bytes 311328 | tf_op jit(solution)/shard_map/ppermute | solution.py:130
  50.1 3.8 %collective-permute-start.3 = (bf16[576,128]{1,0:T(8,128)(2,1)S(1)}, bf16[576,128]{1,0:T(8,128)(2,1)S(1)}, u32[]{:S(2)}, u32[]{:S(2)}) collective-permute-start(bf16[576,128]{1,0:T(8,128)(2,1)S(1)} %slice.42), channel_id=1, source_target_pairs={{0,1},{1,2},{2,3},{3,4},{4,5},{5,6},{6,7},{7,0},{8,9},{9,10},{10,1... | collective-permute-start | bytes 442376 | tf_op jit(solution)/shard_map/ppermute | solution.py:136
  53.9 0.0 collective-permute-done.6.refs_10_
  53.9 0.1 collective-permute-start.7
  54.7 1.9 %collective-permute-done.3.refs_7_ = bf16[576,128]{1,0:T(8,128)(2,1)S(1)} collective-permute-done((bf16[576,128]{1,0:T(8,128)(2,1)S(1)}, bf16[576,128]{1,0:T(8,128)(2,1)S(1)}, u32[]{:S(2)}, u32[]{:S(2)}) %collective-permute-start.3) | collective-permute-done | bytes 147488 | tf_op jit(solution)/shard_map/ppermute | solution.py:136
  56.6 3.8 %collective-permute-done.7.refs_11_ = bf16[576,128]{1,0:T(8,128)(2,1)S(1)} collective-permute-done((bf16[576,128]{1,0:T(8,128)(2,1)S(1)}, bf16[576,128]{1,0:T(8,128)(2,1)S(1)}, u32[]{:S(2)}, u32[]{:S(2)}) %collective-permute-start.7) | collective-permute-done | bytes 147488 | tf_op jit(solution)/shard_map/ppermute | solution.py:137
  60.3 0.0 copy-done.4
  60.4 1.9 %project.1 = (f32[1024,128]{1,0:T(8,128)S(1)}, bf16[1024,128]{1,0:T(8,128)(2,1)S(1)}, bf16[1024,128]{1,0:T(8,128)(2,1)S(1)}) custom-call(s32[1]{0:T(128)} %bitcast.place_ref.refs_0_, bf16[1024,128]{1,0:T(8,128)(2,1)S(1)} %copy-done.2, bf16[128,1024]{1,0:T(8,128)(2,1)S(1)} %bitcast.4, bf16[1024,256]{1,0:T(8,128)(2,1)S(1)} %bitcast.5, ...), custom_call_target="tpu_custom_call" | custom-call | flops 536870912 | bytes 4194304 | tf_op jit(solution)/shard_map/project/pallas_call | solution.py:222
  62.3 10.7 %all-to-all-done.history_ref = bf16[32,4,128,128]{3,2,1,0:T(8,128)(2,1)} async-done(((bf16[32,4,128,128]{3,2,1,0:T(8,128)(2,1)}), bf16[32,4,128,128]{3,2,1,0:T(8,128)(2,1)}, u32[]{:S(2)}, u32[]{:S(2)}) %all-to-all-start) | async-done | bytes 4194336 | tf_op jit(solution)/shard_map/all_to_all | solution.py:364
  72.9 11.1 %attend.2.refs_4_ = bf16[512,128]{1,0:T(8,128)(2,1)S(1)} custom-call(s32[1]{0:T(128)S(6)} %copy.8.count_ref.refs_1_, bf16[1024,128]{1,0:T(8,128)(2,1)S(1)} %get-tuple-element.15.query_ref, f32[1024,128]{1,0:T(8,128)S(1)} %get-tuple-element.16.gate_ref, bf16[32,4,128,128]{3,2,1,0:T(8,128)(2,1)} %all-to-all-done.history_ref), custom_call_target="tpu_custom_call" | custom-call | flops 2147483648 | bytes 4194304 | tf_op jit(solution)/shard_map/attend/pallas_call | solution.py:287
  84.0 3.2 %collective-permute-start.9 = (bf16[512,128]{1,0:T(8,128)(2,1)S(1)}, bf16[512,128]{1,0:T(8,128)(2,1)S(1)}, u32[]{:S(2)}, u32[]{:S(2)}) collective-permute-start(bf16[512,128]{1,0:T(8,128)(2,1)S(1)} %attend.2.refs_4_), channel_id=1, source_target_pairs={{0,1},{1,2},{2,3},{3,4},{4,5},{5,6},{6,7},{7,0},{8,9},{9,10},{10,1... | collective-permute-start | bytes 393224 | tf_op jit(solution)/shard_map/ppermute | solution.py:148
  87.2 0.0 collective-permute-start.8
  87.2 4.7 %attend.3.refs_13_ = bf16[512,128]{1,0:T(8,128)(2,1)S(1)} custom-call(s32[1]{0:T(128)S(6)} %copy.8.count_ref.refs_1_, bf16[1024,128]{1,0:T(8,128)(2,1)S(1)} %get-tuple-element.15.query_ref, f32[1024,128]{1,0:T(8,128)S(1)} %get-tuple-element.16.gate_ref, bf16[32,4,128,128]{3,2,1,0:T(8,128)(2,1)} %all-to-all-done.history_ref), custom_call_target="tpu_custom_call" | custom-call | flops 2147483648 | bytes 4194304 | tf_op jit(solution)/shard_map/attend/pallas_call | solution.py:287
  91.9 3.3 %collective-permute-start.17 = (bf16[512,128]{1,0:T(8,128)(2,1)S(1)}, bf16[512,128]{1,0:T(8,128)(2,1)S(1)}, u32[]{:S(2)}, u32[]{:S(2)}) collective-permute-start(bf16[512,128]{1,0:T(8,128)(2,1)S(1)} %attend.3.refs_13_), channel_id=1, source_target_pairs={{0,1},{1,2},{2,3},{3,4},{4,5},{5,6},{6,7},{7,0},{8,9},{9,10},{10,1... | collective-permute-start | bytes 393224 | tf_op jit(solution)/shard_map/ppermute | solution.py:148
  95.2 0.0 collective-permute-start.16
  95.2 0.0 collective-permute-done.9.refs_6_
  95.2 3.2 %collective-permute-start.11 = (bf16[512,128]{1,0:T(8,128)(2,1)S(1)}, bf16[512,128]{1,0:T(8,128)(2,1)S(1)}, u32[]{:S(2)}, u32[]{:S(2)}) collective-permute-start(bf16[512,128]{1,0:T(8,128)(2,1)S(1)} %collective-permute-done.9.refs_6_), channel_id=1, source_target_pairs={{0,1},{1,2},{2,3},{3,4},{4,5},{5,6},{6,7},{7,0},{8,9},{9,10},{10,1... | collective-permute-start | bytes 393224 | tf_op jit(solution)/shard_map/ppermute | solution.py:148
  98.5 0.0 collective-permute-done.8.refs_5_
  98.5 0.0 collective-permute-start.10
  98.5 0.0 collective-permute-done.17.refs_15_
  98.5 3.6 %collective-permute-start.19 = (bf16[512,128]{1,0:T(8,128)(2,1)S(1)}, bf16[512,128]{1,0:T(8,128)(2,1)S(1)}, u32[]{:S(2)}, u32[]{:S(2)}) collective-permute-start(bf16[512,128]{1,0:T(8,128)(2,1)S(1)} %collective-permute-done.17.refs_15_), channel_id=1, source_target_pairs={{0,1},{1,2},{2,3},{3,4},{4,5},{5,6},{6,7},{7,0},{8,9},{9,10},{10,1... | collective-permute-start | bytes 393224 | tf_op jit(solution)/shard_map/ppermute | solution.py:148
  102.1 0.3 collective-permute-done.16.refs_14_
  102.4 0.0 collective-permute-start.18
  102.4 0.0 collective-permute-done.11.refs_8_
  102.4 3.4 %collective-permute-start.13 = (bf16[512,128]{1,0:T(8,128)(2,1)S(1)}, bf16[512,128]{1,0:T(8,128)(2,1)S(1)}, u32[]{:S(2)}, u32[]{:S(2)}) collective-permute-start(bf16[512,128]{1,0:T(8,128)(2,1)S(1)} %collective-permute-done.11.refs_8_), channel_id=1, source_target_pairs={{0,1},{1,2},{2,3},{3,4},{4,5},{5,6},{6,7},{7,0},{8,9},{9,10},{10,1... | collective-permute-start | bytes 393224 | tf_op jit(solution)/shard_map/ppermute | solution.py:148
  105.8 0.2 collective-permute-done.10.refs_7_
  106.0 0.0 collective-permute-start.12
  106.0 0.0 collective-permute-done.19.refs_17_
  106.0 3.2 %collective-permute-start.21 = (bf16[512,128]{1,0:T(8,128)(2,1)S(1)}, bf16[512,128]{1,0:T(8,128)(2,1)S(1)}, u32[]{:S(2)}, u32[]{:S(2)}) collective-permute-start(bf16[512,128]{1,0:T(8,128)(2,1)S(1)} %collective-permute-done.19.refs_17_), channel_id=1, source_target_pairs={{0,1},{1,2},{2,3},{3,4},{4,5},{5,6},{6,7},{7,0},{8,9},{9,10},{10,1... | collective-permute-start | bytes 393224 | tf_op jit(solution)/shard_map/ppermute | solution.py:148
  109.3 0.0 collective-permute-done.18.refs_16_
  109.3 0.0 collective-permute-start.20
  109.3 0.0 collective-permute-done.13.refs_10_
  109.3 3.3 %collective-permute-start.14 = (bf16[256,128]{1,0:T(8,128)(2,1)S(1)}, bf16[256,128]{1,0:T(8,128)(2,1)S(1)}, u32[]{:S(2)}, u32[]{:S(2)}) collective-permute-start(bf16[256,128]{1,0:T(8,128)(2,1)S(1)} %slice.46), channel_id=1, source_target_pairs={{0,1},{1,2},{2,3},{3,4},{4,5},{5,6},{6,7},{7,0},{8,9},{9,10},{10,1... | collective-permute-start | bytes 196616 | tf_op jit(solution)/shard_map/ppermute | solution.py:152
  112.6 0.1 collective-permute-done.12.refs_9_
  112.7 0.0 collective-permute-start.15
  112.7 0.0 collective-permute-done.21.refs_19_
  112.8 3.3 %collective-permute-start.22 = (bf16[256,128]{1,0:T(8,128)(2,1)S(1)}, bf16[256,128]{1,0:T(8,128)(2,1)S(1)}, u32[]{:S(2)}, u32[]{:S(2)}) collective-permute-start(bf16[256,128]{1,0:T(8,128)(2,1)S(1)} %slice.48), channel_id=1, source_target_pairs={{0,1},{1,2},{2,3},{3,4},{4,5},{5,6},{6,7},{7,0},{8,9},{9,10},{10,1... | collective-permute-start | bytes 196616 | tf_op jit(solution)/shard_map/ppermute | solution.py:152
  116.0 0.0 collective-permute-done.20.refs_18_
  116.1 0.1 collective-permute-start.23
  116.1 0.0 collective-permute-done.14.refs_11_
  116.2 2.0 %collective-permute-done.15.refs_12_ = bf16[256,128]{1,0:T(8,128)(2,1)S(1)} collective-permute-done((bf16[256,128]{1,0:T(8,128)(2,1)S(1)}, bf16[256,128]{1,0:T(8,128)(2,1)S(1)}, u32[]{:S(2)}, u32[]{:S(2)}) %collective-permute-start.15) | collective-permute-done | bytes 65568 | tf_op jit(solution)/shard_map/ppermute | solution.py:153
  118.2 0.0 collective-permute-done.22.refs_20_
  118.2 3.4 %collective-permute-done.23.refs_21_ = bf16[256,128]{1,0:T(8,128)(2,1)S(1)} collective-permute-done((bf16[256,128]{1,0:T(8,128)(2,1)S(1)}, bf16[256,128]{1,0:T(8,128)(2,1)S(1)}, u32[]{:S(2)}, u32[]{:S(2)}) %collective-permute-start.23) | collective-permute-done | bytes 65568 | tf_op jit(solution)/shard_map/ppermute | solution.py:153
  121.6 1.4 %output.1 = bf16[1024,128]{1,0:T(8,128)(2,1)} custom-call(s32[1]{0:T(128)} %bitcast.place_ref.refs_0_, s32[1]{0:T(128)S(6)} %copy.8.count_ref.refs_1_, bf16[1024,128]{1,0:T(8,128)(2,1)S(1)} %copy-done.2, bf16[1024,128]{1,0:T(8,128)(2,1)S(1)} %get-tuple-element.14.refs_3_, bf16[512,128]{1,0:T(8,128)(2,1)S(1)} %attend.2.refs_4_, ...), custom_call_target="tpu_custom_call" | custom-call | flops 268435456 | bytes 4194304 | tf_op jit(solution)/shard_map/output/pallas_call | solution.py:344
  (16 shorter events, 0.1 us)
Async XLA Ops:
  0.0 3.4 %copy-start.1 = (bf16[2,128,128,128]{3,2,1,0:T(8,128)(2,1)S(1)}, bf16[2,128,128,128]{3,2,1,0:T(8,128)(2,1)}, u32[]{:S(2)}) copy-start(bf16[2,128,128,128]{3,2,1,0:T(8,128)(2,1)} %pool_ref.1) | copy-start | bytes 25165828
  3.4 0.7 copy-start.5
  4.0 0.7 copy-start.6
  8.7 2.0 %copy-start = (bf16[32,4,128,128]{3,2,1,0:T(8,128)(2,1)}, bf16[32,4,128,128]{3,2,1,0:T(8,128)(2,1)S(1)}, u32[]{:S(2)}) copy-start(bf16[32,4,128,128]{3,2,1,0:T(8,128)(2,1)S(1)} %pack_live.1) | copy-start | bytes 12582916
  10.7 7.7 %copy-start.2 = (bf16[1024,128]{1,0:T(8,128)(2,1)S(1)}, bf16[1024,128]{1,0:T(8,128)(2,1)}, u32[]{:S(2)}) copy-start(bf16[1024,128]{1,0:T(8,128)(2,1)} %refs_2_.1) | copy-start | bytes 786436
  10.7 7.7 %copy-start.3 = (bf16[1,128,1024]{2,1,0:T(8,128)(2,1)S(1)}, bf16[1,128,1024]{2,1,0:T(8,128)(2,1)}, u32[]{:S(2)}) copy-start(bf16[1,128,1024]{2,1,0:T(8,128)(2,1)} %param.9) | copy-start | bytes 786436
  10.7 49.6 %copy-start.4 = (bf16[1024,1,256]{2,0,1:T(8,128)(2,1)S(1)}, bf16[1024,1,256]{2,0,1:T(8,128)(2,1)}, u32[]{:S(2)}) copy-start(bf16[1024,1,256]{2,0,1:T(8,128)(2,1)} %param.8) | copy-start | bytes 1572868
  10.7 62.2 %all-to-all-start = ((bf16[32,4,128,128]{3,2,1,0:T(8,128)(2,1)}), bf16[32,4,128,128]{3,2,1,0:T(8,128)(2,1)}, u32[]{:S(2)}, u32[]{:S(2)}) async-start(bf16[32,4,128,128]{3,2,1,0:T(8,128)(2,1)} %copy-done), calls=%async_computation | async-start | bytes 8388608 | tf_op jit(solution)/shard_map/all_to_all | solution.py:364
  18.7 11.5 %collective-permute-start = (bf16[1472,128]{1,0:T(8,128)(2,1)S(1)}, bf16[1472,128]{1,0:T(8,128)(2,1)S(1)}, u32[]{:S(2)}, u32[]{:S(2)}) collective-permute-start(bf16[1472,128]{1,0:T(8,128)(2,1)S(1)} %get-tuple-element.12), channel_id=1, source_target_pairs={{0,1},{1,2},{2,3},{3,4},{4,5},{5,6},{6,7},{7,0},{8,9},{9,10},{10,1... | collective-permute-start | bytes 1130504 | tf_op jit(solution)/shard_map/ppermute | solution.py:130
  21.9 12.1 %collective-permute-start.4 = (bf16[1472,128]{1,0:T(8,128)(2,1)S(1)}, bf16[1472,128]{1,0:T(8,128)(2,1)S(1)}, u32[]{:S(2)}, u32[]{:S(2)}) collective-permute-start(bf16[1472,128]{1,0:T(8,128)(2,1)S(1)} %get-tuple-element.13), channel_id=1, source_target_pairs={{0,7},{1,0},{2,1},{3,2},{4,3},{5,4},{6,5},{7,6},{8,15},{9,8},{10,9... | collective-permute-start | bytes 1130504 | tf_op jit(solution)/shard_map/ppermute | solution.py:131
  30.2 10.7 %collective-permute-start.1 = (bf16[1344,128]{1,0:T(8,128)(2,1)S(1)}, bf16[1344,128]{1,0:T(8,128)(2,1)S(1)}, u32[]{:S(2)}, u32[]{:S(2)}) collective-permute-start(bf16[1344,128]{1,0:T(8,128)(2,1)S(1)} %slice.40), channel_id=1, source_target_pairs={{0,1},{1,2},{2,3},{3,4},{4,5},{5,6},{6,7},{7,0},{8,9},{9,10},{10,1... | collective-permute-start | bytes 1032200 | tf_op jit(solution)/shard_map/ppermute | solution.py:130
  34.0 10.7 %collective-permute-start.5 = (bf16[1344,128]{1,0:T(8,128)(2,1)S(1)}, bf16[1344,128]{1,0:T(8,128)(2,1)S(1)}, u32[]{:S(2)}, u32[]{:S(2)}) collective-permute-start(bf16[1344,128]{1,0:T(8,128)(2,1)S(1)} %slice.43), channel_id=1, source_target_pairs={{0,7},{1,0},{2,1},{3,2},{4,3},{5,4},{6,5},{7,6},{8,15},{9,8},{10,9... | collective-permute-start | bytes 1032200 | tf_op jit(solution)/shard_map/ppermute | solution.py:131
  41.0 9.2 %collective-permute-start.2 = (bf16[1216,128]{1,0:T(8,128)(2,1)S(1)}, bf16[1216,128]{1,0:T(8,128)(2,1)S(1)}, u32[]{:S(2)}, u32[]{:S(2)}) collective-permute-start(bf16[1216,128]{1,0:T(8,128)(2,1)S(1)} %slice.41), channel_id=1, source_target_pairs={{0,1},{1,2},{2,3},{3,4},{4,5},{5,6},{6,7},{7,0},{8,9},{9,10},{10,1... | collective-permute-start | bytes 933896 | tf_op jit(solution)/shard_map/ppermute | solution.py:130
  44.8 9.1 %collective-permute-start.6 = (bf16[1216,128]{1,0:T(8,128)(2,1)S(1)}, bf16[1216,128]{1,0:T(8,128)(2,1)S(1)}, u32[]{:S(2)}, u32[]{:S(2)}) collective-permute-start(bf16[1216,128]{1,0:T(8,128)(2,1)S(1)} %slice.44), channel_id=1, source_target_pairs={{0,7},{1,0},{2,1},{3,2},{4,3},{5,4},{6,5},{7,6},{8,15},{9,8},{10,9... | collective-permute-start | bytes 933896 | tf_op jit(solution)/shard_map/ppermute | solution.py:131
  50.1 6.4 %collective-permute-start.3 = (bf16[576,128]{1,0:T(8,128)(2,1)S(1)}, bf16[576,128]{1,0:T(8,128)(2,1)S(1)}, u32[]{:S(2)}, u32[]{:S(2)}) collective-permute-start(bf16[576,128]{1,0:T(8,128)(2,1)S(1)} %slice.42), channel_id=1, source_target_pairs={{0,1},{1,2},{2,3},{3,4},{4,5},{5,6},{6,7},{7,0},{8,9},{9,10},{10,1... | collective-permute-start | bytes 442376 | tf_op jit(solution)/shard_map/ppermute | solution.py:136
  53.9 6.4 %collective-permute-start.7 = (bf16[576,128]{1,0:T(8,128)(2,1)S(1)}, bf16[576,128]{1,0:T(8,128)(2,1)S(1)}, u32[]{:S(2)}, u32[]{:S(2)}) collective-permute-start(bf16[576,128]{1,0:T(8,128)(2,1)S(1)} %slice.45), channel_id=1, source_target_pairs={{0,7},{1,0},{2,1},{3,2},{4,3},{5,4},{6,5},{7,6},{8,15},{9,8},{10,9... | collective-permute-start | bytes 442376 | tf_op jit(solution)/shard_map/ppermute | solution.py:137
  84.0 11.2 %collective-permute-start.9 = (bf16[512,128]{1,0:T(8,128)(2,1)S(1)}, bf16[512,128]{1,0:T(8,128)(2,1)S(1)}, u32[]{:S(2)}, u32[]{:S(2)}) collective-permute-start(bf16[512,128]{1,0:T(8,128)(2,1)S(1)} %attend.2.refs_4_), channel_id=1, source_target_pairs={{0,1},{1,2},{2,3},{3,4},{4,5},{5,6},{6,7},{7,0},{8,9},{9,10},{10,1... | collective-permute-start | bytes 393224 | tf_op jit(solution)/shard_map/ppermute | solution.py:148
  87.2 11.3 %collective-permute-start.8 = (bf16[512,128]{1,0:T(8,128)(2,1)S(1)}, bf16[512,128]{1,0:T(8,128)(2,1)S(1)}, u32[]{:S(2)}, u32[]{:S(2)}) collective-permute-start(bf16[512,128]{1,0:T(8,128)(2,1)S(1)} %attend.2.refs_4_), channel_id=1, source_target_pairs={{0,7},{1,0},{2,1},{3,2},{4,3},{5,4},{6,5},{7,6},{8,15},{9,8},{10,9... | collective-permute-start | bytes 393224 | tf_op jit(solution)/shard_map/ppermute | solution.py:149
  91.9 6.6 %collective-permute-start.17 = (bf16[512,128]{1,0:T(8,128)(2,1)S(1)}, bf16[512,128]{1,0:T(8,128)(2,1)S(1)}, u32[]{:S(2)}, u32[]{:S(2)}) collective-permute-start(bf16[512,128]{1,0:T(8,128)(2,1)S(1)} %attend.3.refs_13_), channel_id=1, source_target_pairs={{0,1},{1,2},{2,3},{3,4},{4,5},{5,6},{6,7},{7,0},{8,9},{9,10},{10,1... | collective-permute-start | bytes 393224 | tf_op jit(solution)/shard_map/ppermute | solution.py:148
  95.2 7.1 %collective-permute-start.16 = (bf16[512,128]{1,0:T(8,128)(2,1)S(1)}, bf16[512,128]{1,0:T(8,128)(2,1)S(1)}, u32[]{:S(2)}, u32[]{:S(2)}) collective-permute-start(bf16[512,128]{1,0:T(8,128)(2,1)S(1)} %attend.3.refs_13_), channel_id=1, source_target_pairs={{0,7},{1,0},{2,1},{3,2},{4,3},{5,4},{6,5},{7,6},{8,15},{9,8},{10,9... | collective-permute-start | bytes 393224 | tf_op jit(solution)/shard_map/ppermute | solution.py:149
  95.2 7.1 %collective-permute-start.11 = (bf16[512,128]{1,0:T(8,128)(2,1)S(1)}, bf16[512,128]{1,0:T(8,128)(2,1)S(1)}, u32[]{:S(2)}, u32[]{:S(2)}) collective-permute-start(bf16[512,128]{1,0:T(8,128)(2,1)S(1)} %collective-permute-done.9.refs_6_), channel_id=1, source_target_pairs={{0,1},{1,2},{2,3},{3,4},{4,5},{5,6},{6,7},{7,0},{8,9},{9,10},{10,1... | collective-permute-start | bytes 393224 | tf_op jit(solution)/shard_map/ppermute | solution.py:148
  98.5 7.5 %collective-permute-start.10 = (bf16[512,128]{1,0:T(8,128)(2,1)S(1)}, bf16[512,128]{1,0:T(8,128)(2,1)S(1)}, u32[]{:S(2)}, u32[]{:S(2)}) collective-permute-start(bf16[512,128]{1,0:T(8,128)(2,1)S(1)} %collective-permute-done.8.refs_5_), channel_id=1, source_target_pairs={{0,7},{1,0},{2,1},{3,2},{4,3},{5,4},{6,5},{7,6},{8,15},{9,8},{10,9... | collective-permute-start | bytes 393224 | tf_op jit(solution)/shard_map/ppermute | solution.py:149
  98.5 7.5 %collective-permute-start.19 = (bf16[512,128]{1,0:T(8,128)(2,1)S(1)}, bf16[512,128]{1,0:T(8,128)(2,1)S(1)}, u32[]{:S(2)}, u32[]{:S(2)}) collective-permute-start(bf16[512,128]{1,0:T(8,128)(2,1)S(1)} %collective-permute-done.17.refs_15_), channel_id=1, source_target_pairs={{0,1},{1,2},{2,3},{3,4},{4,5},{5,6},{6,7},{7,0},{8,9},{9,10},{10,1... | collective-permute-start | bytes 393224 | tf_op jit(solution)/shard_map/ppermute | solution.py:148
  102.4 6.9 %collective-permute-start.18 = (bf16[512,128]{1,0:T(8,128)(2,1)S(1)}, bf16[512,128]{1,0:T(8,128)(2,1)S(1)}, u32[]{:S(2)}, u32[]{:S(2)}) collective-permute-start(bf16[512,128]{1,0:T(8,128)(2,1)S(1)} %collective-permute-done.16.refs_14_), channel_id=1, source_target_pairs={{0,7},{1,0},{2,1},{3,2},{4,3},{5,4},{6,5},{7,6},{8,15},{9,8},{10,9... | collective-permute-start | bytes 393224 | tf_op jit(solution)/shard_map/ppermute | solution.py:149
  102.4 6.9 %collective-permute-start.13 = (bf16[512,128]{1,0:T(8,128)(2,1)S(1)}, bf16[512,128]{1,0:T(8,128)(2,1)S(1)}, u32[]{:S(2)}, u32[]{:S(2)}) collective-permute-start(bf16[512,128]{1,0:T(8,128)(2,1)S(1)} %collective-permute-done.11.refs_8_), channel_id=1, source_target_pairs={{0,1},{1,2},{2,3},{3,4},{4,5},{5,6},{6,7},{7,0},{8,9},{9,10},{10,1... | collective-permute-start | bytes 393224 | tf_op jit(solution)/shard_map/ppermute | solution.py:148
  106.0 6.7 %collective-permute-start.12 = (bf16[512,128]{1,0:T(8,128)(2,1)S(1)}, bf16[512,128]{1,0:T(8,128)(2,1)S(1)}, u32[]{:S(2)}, u32[]{:S(2)}) collective-permute-start(bf16[512,128]{1,0:T(8,128)(2,1)S(1)} %collective-permute-done.10.refs_7_), channel_id=1, source_target_pairs={{0,7},{1,0},{2,1},{3,2},{4,3},{5,4},{6,5},{7,6},{8,15},{9,8},{10,9... | collective-permute-start | bytes 393224 | tf_op jit(solution)/shard_map/ppermute | solution.py:149
  106.0 6.7 %collective-permute-start.21 = (bf16[512,128]{1,0:T(8,128)(2,1)S(1)}, bf16[512,128]{1,0:T(8,128)(2,1)S(1)}, u32[]{:S(2)}, u32[]{:S(2)}) collective-permute-start(bf16[512,128]{1,0:T(8,128)(2,1)S(1)} %collective-permute-done.19.refs_17_), channel_id=1, source_target_pairs={{0,1},{1,2},{2,3},{3,4},{4,5},{5,6},{6,7},{7,0},{8,9},{9,10},{10,1... | collective-permute-start | bytes 393224 | tf_op jit(solution)/shard_map/ppermute | solution.py:148
  109.3 6.8 %collective-permute-start.20 = (bf16[512,128]{1,0:T(8,128)(2,1)S(1)}, bf16[512,128]{1,0:T(8,128)(2,1)S(1)}, u32[]{:S(2)}, u32[]{:S(2)}) collective-permute-start(bf16[512,128]{1,0:T(8,128)(2,1)S(1)} %collective-permute-done.18.refs_16_), channel_id=1, source_target_pairs={{0,7},{1,0},{2,1},{3,2},{4,3},{5,4},{6,5},{7,6},{8,15},{9,8},{10,9... | collective-permute-start | bytes 393224 | tf_op jit(solution)/shard_map/ppermute | solution.py:149
  109.3 6.9 %collective-permute-start.14 = (bf16[256,128]{1,0:T(8,128)(2,1)S(1)}, bf16[256,128]{1,0:T(8,128)(2,1)S(1)}, u32[]{:S(2)}, u32[]{:S(2)}) collective-permute-start(bf16[256,128]{1,0:T(8,128)(2,1)S(1)} %slice.46), channel_id=1, source_target_pairs={{0,1},{1,2},{2,3},{3,4},{4,5},{5,6},{6,7},{7,0},{8,9},{9,10},{10,1... | collective-permute-start | bytes 196616 | tf_op jit(solution)/shard_map/ppermute | solution.py:152
  112.7 5.5 %collective-permute-start.15 = (bf16[256,128]{1,0:T(8,128)(2,1)S(1)}, bf16[256,128]{1,0:T(8,128)(2,1)S(1)}, u32[]{:S(2)}, u32[]{:S(2)}) collective-permute-start(bf16[256,128]{1,0:T(8,128)(2,1)S(1)} %slice.47), channel_id=1, source_target_pairs={{0,7},{1,0},{2,1},{3,2},{4,3},{5,4},{6,5},{7,6},{8,15},{9,8},{10,9... | collective-permute-start | bytes 196616 | tf_op jit(solution)/shard_map/ppermute | solution.py:153
  112.8 5.4 %collective-permute-start.22 = (bf16[256,128]{1,0:T(8,128)(2,1)S(1)}, bf16[256,128]{1,0:T(8,128)(2,1)S(1)}, u32[]{:S(2)}, u32[]{:S(2)}) collective-permute-start(bf16[256,128]{1,0:T(8,128)(2,1)S(1)} %slice.48), channel_id=1, source_target_pairs={{0,1},{1,2},{2,3},{3,4},{4,5},{5,6},{6,7},{7,0},{8,9},{9,10},{10,1... | collective-permute-start | bytes 196616 | tf_op jit(solution)/shard_map/ppermute | solution.py:152
  116.1 5.6 %collective-permute-start.23 = (bf16[256,128]{1,0:T(8,128)(2,1)S(1)}, bf16[256,128]{1,0:T(8,128)(2,1)S(1)}, u32[]{:S(2)}, u32[]{:S(2)}) collective-permute-start(bf16[256,128]{1,0:T(8,128)(2,1)S(1)} %slice.49), channel_id=1, source_target_pairs={{0,7},{1,0},{2,1},{3,2},{4,3},{5,4},{6,5},{7,6},{8,15},{9,8},{10,9... | collective-permute-start | bytes 196616 | tf_op jit(solution)/shard_map/ppermute | solution.py:153
